TPU v7x, 32 devices: a whole 2x2x4 slice. The times are simulated.
32 devices in a mesh: ta: 2 (over y), gx: 4 (over x, core), yz: 4 (over z).
Axes of the slice: x: 2, y: 2, z: 4, core: 2. Of those that a mesh axis runs over, the one named last changes fastest.
Arguments:
- vectors: bfloat16 [2, 3, 32, 32, 64, 128], P(None, None, 'gx', 'yz', 'ta'), parts along dimension 4, may hold values from -6 to 6
- gauge_x: float32 [2, 3, 3, 32, 32, 64], P(None, None, None, 'gx', 'yz', 'ta'), parts along dimension 5, may hold values from -6 to 6
- gauge_y: float32 [2, 3, 3, 32, 32, 64], P(None, None, None, 'gx', 'yz', 'ta'), parts along dimension 5, may hold values from -6 to 6
Outputs:
- elementals: float32 [4, 2, 128, 128], P('ta'), parts along dimension 0
There are 2 independent parts, one for each index of `ta`. A program takes and returns all parts, laid end to end along the dimension named above; each array names one. Nothing has to cross between parts.
All inputs are finite; a program needn't handle non-finite values.
Results may differ from a plain program's by a relative error of at most 0.0029.
Values may be sent and summed in bfloat16 or wider, within the bound.
A program may use at most 64 MiB of HBM per device.

v0:
```python
import math

import jax
import jax.numpy as jnp
from jax import lax
from jax.sharding import PartitionSpec as P


def shifted(value, axis, steps):
    count = lax.axis_size(axis)
    pairs = [(source, (source + steps) % count) for source in range(count)]
    return lax.ppermute(value, axis, pairs)


def colour_apply(gauge, source_vectors):
    real_parts = []
    imag_parts = []
    for colour in range(3):
        real_running = jnp.zeros(source_vectors.shape[2:], jnp.float32)
        imaginary_running = jnp.zeros(source_vectors.shape[2:], jnp.float32)
        for inner_product in range(3):
            left_real = gauge[0, colour, inner_product][..., None]
            left_imaginary = gauge[1, colour, inner_product][..., None]
            right_real = source_vectors[0, inner_product].astype(jnp.float32)
            right_imaginary = source_vectors[1, inner_product].astype(jnp.float32)
            real_running = real_running + left_real * right_real - left_imaginary * right_imaginary
            imaginary_running = (
                imaginary_running + left_real * right_imaginary + left_imaginary * right_real
            )
        real_parts.append(real_running)
        imag_parts.append(imaginary_running)
    return jnp.stack([jnp.stack(real_parts), jnp.stack(imag_parts)]).astype(jnp.bfloat16)


def right_block(image):
    nvecs = image.shape[-1]
    real_rows = image[0].reshape(-1, nvecs)
    imag_rows = image[1].reshape(-1, nvecs)
    first = jnp.concatenate([real_rows, imag_rows], 0)
    second = jnp.concatenate([imag_rows, -real_rows], 0)
    return (first, second)


def contract(left_cols, right_cols):
    return lax.dot_general(
        left_cols, right_cols, (((0,), (0,)), ((), ())), preferred_element_type=jnp.float32
    )


def local(vectors, gauge_x, gauge_y):
    nvecs = vectors.shape[-1]
    from_next_x = shifted(vectors[:, :, :1], "gx", -1)
    shifted_x = jnp.concatenate([vectors[:, :, 1:], from_next_x], 2)
    from_next_y = shifted(vectors[:, :, :, :1], "yz", -1)
    shifted_y = jnp.concatenate([vectors[:, :, :, 1:], from_next_y], 3)
    image_x = colour_apply(gauge_x, shifted_x)
    image_y = colour_apply(gauge_y, shifted_y)
    left_rows = vectors.reshape(-1, nvecs)
    blocks = right_block(image_x) + right_block(image_y)
    summed = lax.psum(
        jnp.concatenate([contract(left_rows, member) for member in blocks], 1), ("gx", "yz")
    )
    sites_total = (
        vectors.shape[2]
        * lax.axis_size("gx")
        * vectors.shape[3]
        * lax.axis_size("yz")
        * vectors.shape[4]
    )
    scaling = 1.0 / math.sqrt(3.0 * sites_total)
    return (summed * scaling).reshape(nvecs, 2, 2, nvecs).transpose(1, 2, 0, 3)


def solution(mesh):
    placed = (
        P(None, None, "gx", "yz", "ta", None),
        P(None, None, None, "gx", "yz", "ta"),
        P(None, None, None, "gx", "yz", "ta"),
    )
    return jax.shard_map(
        local, mesh=mesh, in_specs=placed, out_specs=P("ta", None, None, None), check_vma=False
    )
```

profile of v0, /device:TPU:0, one launch (start us, length us, event | category | flops | bytes accessed | tf_op | source)
XLA Modules:
  0.0 137.0 jit_solution(17491967884599088019)
XLA Ops:
  6.5 0.0 all-reduce.2.cloned.1.call-start
  6.5 1.0 slice.186
  7.6 0.0 copy-start
  7.6 2.4 %collective-permute-start = (bf16[2,3,1,8,32,128]{5,4,3,2,1,0:T(8,128)(2,1)S(1)}, bf16[2,3,1,8,32,128]{5,4,3,2,1,0:T(8,128)(2,1)S(1)}, u32[]{:S(2)}, u32[]{:S(2)}) collective-permute-start(bf16[2,3,1,8,32,128]{5,4,3,2,1,0:T(8,128)(2,1)S(1)} %slice.186), channel_id=1, source_target_pairs={{0,12},{4,0},{8,4},{12,8},{1,13},{5,1},{9,5},{13,9},{2,14},{6,2},{... | collective-permute-start | bytes 1179656 | tf_op jit(solution)/shard_map/ppermute | solution.py:12
  10.0 1.0 slice.212
  11.0 3.7 %collective-permute-start.1 = (bf16[2,3,8,1,32,128]{5,4,3,2,1,0:T(8,128)(2,1)S(1)}, bf16[2,3,8,1,32,128]{5,4,3,2,1,0:T(8,128)(2,1)S(1)}, u32[]{:S(2)}, u32[]{:S(2)}) collective-permute-start(bf16[2,3,8,1,32,128]{5,4,3,2,1,0:T(8,128)(2,1)S(1)} %slice.212), channel_id=1, source_target_pairs={{0,3},{1,0},{2,1},{3,2},{4,7},{5,4},{6,5},{7,6},{8,11},{9,8},{10,9... | collective-permute-start | bytes 1179656 | tf_op jit(solution)/shard_map/ppermute | solution.py:12
  14.7 0.0 copy-done
  14.7 0.0 copy-start.1
  14.7 0.0 copy-start.2
  14.7 0.0 slice-start
  14.7 0.7 slice.211
  15.4 0.4 copy-done.1
  15.8 0.1 copy-done.2
  16.0 0.0 collective-permute-done
  16.0 0.8 slice-done
  16.8 2.1 %fusion.51 = (bf16[1,8,8,32,128]{4,3,2,1,0:T(8,128)(2,1)S(1)}, bf16[1,8,8,32,128]{4,3,2,1,0:T(8,128)(2,1)S(1)}, bf16[1,8,8,32,128]{4,3,2,1,0:T(8,128)(2,1)S(1)},...) fusion(f32[8,8,32]{2,1,0:T(8,128)S(1)} %get-tuple-element.41, ...), kind=kLoop, calls=%fused_computation.139 | loop fusion | flops 6291456 | bytes 6864896 | tf_op jit(solution)/shard_map/convert.25
  18.9 1.9 %fusion.33 = bf16[1,8,8,32,128]{4,3,2,1,0:T(8,128)(2,1)S(1)} fusion(bf16[1,8,8,32,128]{4,3,2,1,0:T(8,128)(2,1)S(1)} %get-tuple-element.11, bf16[1,8,8,32,128]{4,3,2,1,0:T(8,128)(2,1)S(1)} %get-tuple-element.10, bf16[1,8,8,32,128]{4,3,2,1,0:T(8,128)(2,1)S(1)} %get-tuple-element.9, bf16[1,8,8,32,128]{4,3,2,1,0:T(8,128)(2,1)S(1)} %get-tuple-element.8, ...), kind=kLoop, calls=%fused_computation.121 | loop fusion | flops 4718592 | bytes 3719168 | tf_op jit(solution)/shard_map/convert.29
  20.9 3.9 %fusion.57 = (bf16[1,8,8,32,128]{4,3,2,1,0:T(8,128)(2,1)S(1)}, bf16[1,8,8,32,128]{4,3,2,1,0:T(8,128)(2,1)S(1)}, bf16[1,8,8,32,128]{4,3,2,1,0:T(8,128)(2,1)S(1)}, bf16[1,8,8,32,128]{4,3,2,1,0:T(8,128)(2,1)S(1)}) fusion(bf16[1,8,8,32,128]{4,3,2,1,0:T(8,128)(2,1)S(1)} %get-tuple-element.11, bf16[1,8,8,32,128]{4,3,2,1,0:T(8,128)(2,1)S(1)} %get-tuple-element.10, ...), kind=kLoop, calls=%fused_computation.145 | loop fusion | flops 14155776 | bytes 5341184 | tf_op jit(solution)/shard_map/convert.26
  24.8 0.3 pad_maximum_fusion
  25.1 0.3 bitcast_negate_fusion.1
  25.4 1.0 fusion.25
  26.5 1.0 fusion.22
  27.5 0.0 collective-permute-done.1
  27.5 2.0 %fusion.87 = (bf16[1,8,8,32,128]{4,3,2,1,0:T(8,128)(2,1)S(1)}, bf16[1,8,8,32,128]{4,3,2,1,0:T(8,128)(2,1)S(1)}, bf16[1,8,8,32,128]{4,3,2,1,0:T(8,128)(2,1)S(1)},...) fusion(f32[8,8,32]{2,1,0:T(8,128)S(1)} %get-tuple-element.59, ...), kind=kLoop, calls=%fused_computation.175 | loop fusion | flops 6291456 | bytes 6864896 | tf_op jit(solution)/shard_map/convert.15
  29.6 1.9 %fusion.69 = bf16[1,8,8,32,128]{4,3,2,1,0:T(8,128)(2,1)S(1)} fusion(bf16[1,8,8,32,128]{4,3,2,1,0:T(8,128)(2,1)S(1)} %get-tuple-element.18, bf16[1,8,8,32,128]{4,3,2,1,0:T(8,128)(2,1)S(1)} %get-tuple-element.17, bf16[1,8,8,32,128]{4,3,2,1,0:T(8,128)(2,1)S(1)} %get-tuple-element.16, bf16[1,8,8,32,128]{4,3,2,1,0:T(8,128)(2,1)S(1)} %get-tuple-element.15, ...), kind=kLoop, calls=%fused_computation.157 | loop fusion | flops 4718592 | bytes 3719168 | tf_op jit(solution)/shard_map/convert.19
  31.5 3.9 %fusion.93 = (bf16[1,8,8,32,128]{4,3,2,1,0:T(8,128)(2,1)S(1)}, bf16[1,8,8,32,128]{4,3,2,1,0:T(8,128)(2,1)S(1)}, bf16[1,8,8,32,128]{4,3,2,1,0:T(8,128)(2,1)S(1)}, bf16[1,8,8,32,128]{4,3,2,1,0:T(8,128)(2,1)S(1)}) fusion(bf16[1,8,8,32,128]{4,3,2,1,0:T(8,128)(2,1)S(1)} %get-tuple-element.18, bf16[1,8,8,32,128]{4,3,2,1,0:T(8,128)(2,1)S(1)} %get-tuple-element.17, ...), kind=kLoop, calls=%fused_computation.181 | loop fusion | flops 14155776 | bytes 5341184 | tf_op jit(solution)/shard_map/convert.16
  35.4 0.3 pad_maximum_fusion.2
  35.8 0.3 bitcast_negate_fusion
  36.1 1.0 fusion.19
  37.1 1.1 fusion.16
  38.2 0.7 pad_maximum_fusion.6
  38.9 0.0 all-reduce.2.cloned.1.call-update
  39.0 89.4 %all-reduce.2.cloned.1.call-done = f32[128,512]{0,1:T(8,128)} async-done(((f32[128,512]{0,1:T(8,128)}), f32[128,512]{0,1:T(8,128)}) %all-reduce.2.cloned.1.call-update) | async-done | bytes 262160 | tf_op jit(solution)/shard_map/psum | solution.py:60
  128.4 1.0 broadcast_multiply_fusion
  129.4 0.8 copy.4
  (2 shorter events, 0.1 us)
Async XLA Ops:
  6.5 121.8 %all-reduce.2.cloned.1.call-start = ((), (), s32[]{:S(2)}) async-start(), calls=%async_computation | async-start | bytes 524288 | tf_op jit(solution)/shard_map/psum | solution.py:60
  7.6 7.1 %copy-start = (bf16[2,3,8,8,32,128]{5,4,3,2,1,0:T(8,128)(2,1)S(1)}, bf16[2,3,8,8,32,128]{5,4,3,2,1,0:T(8,128)(2,1)}, u32[]{:S(2)}) copy-start(bf16[2,3,8,8,32,128]{5,4,3,2,1,0:T(8,128)(2,1)} %param.3) | copy-start | bytes 9437188
  7.6 8.4 %collective-permute-start = (bf16[2,3,1,8,32,128]{5,4,3,2,1,0:T(8,128)(2,1)S(1)}, bf16[2,3,1,8,32,128]{5,4,3,2,1,0:T(8,128)(2,1)S(1)}, u32[]{:S(2)}, u32[]{:S(2)}) collective-permute-start(bf16[2,3,1,8,32,128]{5,4,3,2,1,0:T(8,128)(2,1)S(1)} %slice.186), channel_id=1, source_target_pairs={{0,12},{4,0},{8,4},{12,8},{1,13},{5,1},{9,5},{13,9},{2,14},{6,2},{... | collective-permute-start | bytes 1179656 | tf_op jit(solution)/shard_map/ppermute | solution.py:12
  11.0 16.5 %collective-permute-start.1 = (bf16[2,3,8,1,32,128]{5,4,3,2,1,0:T(8,128)(2,1)S(1)}, bf16[2,3,8,1,32,128]{5,4,3,2,1,0:T(8,128)(2,1)S(1)}, u32[]{:S(2)}, u32[]{:S(2)}) collective-permute-start(bf16[2,3,8,1,32,128]{5,4,3,2,1,0:T(8,128)(2,1)S(1)} %slice.212), channel_id=1, source_target_pairs={{0,3},{1,0},{2,1},{3,2},{4,7},{5,4},{6,5},{7,6},{8,11},{9,8},{10,9... | collective-permute-start | bytes 1179656 | tf_op jit(solution)/shard_map/ppermute | solution.py:12
  14.7 1.1 copy-start.1
  14.7 1.2 copy-start.2
  14.7 2.1 %slice-start = ((bf16[2,3,8,8,32,128]{5,4,3,2,1,0:T(8,128)(2,1)}), bf16[2,3,7,8,32,128]{5,4,3,2,1,0:T(8,128)(2,1)S(1)}, s32[]{:S(2)}) async-start(bf16[2,3,8,8,32,128]{5,4,3,2,1,0:T(8,128)(2,1)} %param.3), calls=%async_computation.1 | async-start | bytes 5505024 | tf_op jit(solution)/shard_map/slice | solution.py:53
Sparse Core Ops, SparseCore 0:
  39.1 89.2 all-reduce.1
where the time goes:
time: 137 us
  waiting for transfers between devices  89.4 us (65%)
  other arithmetic  18.8 us (14%)
  between operations  13.6 us (10%)
  starting transfers between devices  6.09 us (4%)
  local copies, waits for them, and re-layouts  5 us (4%)
  matrix products  4.18 us (3%)
    psum x1, waiting for transfers between devices, local(): lax.psum(jnp.concatenate([contract(left_rows, member) for member in block...  89.4 us
    another operation x6, other arithmetic  15.8 us
    ppermute x2, starting transfers between devices, shifted(): return lax.ppermute(value, axis, pairs)  6.08 us
    dot_general x4, matrix products, contract(): lax.dot_general(left_cols, right_cols, (((0,), (0,)), ((), ())), preferre...  4.18 us
  transfers between devices with their start and end apart: 3, of which 1 were waited for; matrix products, arithmetic and copies ran while one was open for 9% of the time, Pallas kernels for 0%

commit v1 on v0

v1 whole, which is shorter than its diff:
```python
import functools
import math

import jax
import jax.numpy as jnp
from jax import lax
from jax.experimental import pallas as pl
from jax.experimental.pallas import tpu as pltpu
from jax.sharding import PartitionSpec as P

MESH = pl.DeviceIdType.MESH


def kernel(
    ngx, nyz, scaling,
    v_hbm, gx_hbm, gy_hbm, out_ref,
    v, hy, gauge, vt, acc, part, landed,
    load_sem, gauge_sem, halo_send, halo_recv, rs_send, rs_recv, ag_send, ag_recv,
):
    nx, ny, nz, nv = v_hbm.shape[2:]
    rows = 3 * nz
    ranks = ngx * nyz
    chunk = 2 * nv // ranks
    my_x = lax.axis_index("gx")
    my_y = lax.axis_index("yz")
    me = my_x * nyz + my_y

    def gauge_copy(d):
        return pltpu.make_async_copy((gx_hbm, gy_hbm)[d], gauge.at[d], gauge_sem.at[d])

    def row_copy(x):
        return pltpu.make_async_copy(v_hbm.at[:, :, x], v.at[:, :, x], load_sem.at[x])

    gauge_copy(0).start()
    for x in range(nx):
        row_copy(x).start()
    gauge_copy(1).start()

    def peer(k):
        kx, ky = k // nyz, k % nyz
        return lax.rem(my_x + kx, ngx), lax.rem(my_y + ky, nyz)

    barrier = pltpu.get_barrier_semaphore()
    for k in range(1, ranks):
        px, py = peer(k)
        pl.semaphore_signal(
            barrier, inc=1, device_id={"gx": px, "yz": py}, device_id_type=MESH
        )
    pl.semaphore_wait(barrier, ranks - 1)

    halo_x = pltpu.make_async_remote_copy(
        src_ref=v_hbm.at[:, :, 0], dst_ref=v.at[:, :, nx],
        send_sem=halo_send.at[0], recv_sem=halo_recv.at[0],
        device_id={"gx": lax.rem(my_x + ngx - 1, ngx)}, device_id_type=MESH,
    )
    halo_y = pltpu.make_async_remote_copy(
        src_ref=v_hbm.at[:, :, :, 0], dst_ref=hy,
        send_sem=halo_send.at[1], recv_sem=halo_recv.at[1],
        device_id={"yz": lax.rem(my_y + nyz - 1, nyz)}, device_id_type=MESH,
    )
    halo_x.start()
    halo_y.start()

    lanes = lax.broadcasted_iota(jnp.int32, (nz, 2 * rows), 1) % nz
    subs = lax.broadcasted_iota(jnp.int32, (nz, 2 * rows), 0)
    diagonal = jnp.where(lanes == subs, 1.0, 0.0).astype(jnp.bfloat16)

    def links(d, x):
        found = []
        for a in range(3):
            pieces = [gauge[d, r, a, b, x] for r in range(2) for b in range(3)]
            full = jnp.concatenate(pieces, axis=1)
            high = full.astype(jnp.bfloat16).astype(jnp.float32)
            found.append((high, full - high))
        return found

    def spread(row):
        wide = jnp.broadcast_to(row, (nz, 2 * rows)).astype(jnp.bfloat16)
        return wide * diagonal

    def image(found, y, source):
        real = source[0].reshape(rows, nv)
        imag = source[1].reshape(rows, nv)
        weights = jnp.concatenate(
            [jnp.concatenate([real, -imag], 0), jnp.concatenate([imag, real], 0)], 1
        )
        parts = [spread(found[a][p][y : y + 1]) for p in range(2) for a in range(3)]
        both = jnp.dot(
            jnp.concatenate(parts, 0), weights, preferred_element_type=jnp.float32
        )
        return (both[:rows] + both[rows:]).astype(jnp.bfloat16)

    def left(sites):
        return jnp.concatenate(
            [
                jnp.concatenate([v[r, :, x, y].reshape(rows, nv) for x, y in sites], 0)
                for r in range(2)
            ],
            1,
        )

    def finish(d):
        total = acc[...]
        part[d, :nv] = total[:nv, :nv] + total[nv:, nv:]
        part[d, nv:] = total[:nv, nv:] - total[nv:, :nv]

    def scatter(d, k):
        px, py = peer(k)
        owner = px * nyz + py
        return pltpu.make_async_remote_copy(
            src_ref=part.at[d, pl.ds(pl.multiple_of(owner * chunk, chunk), chunk)],
            dst_ref=landed.at[d, k],
            send_sem=rs_send.at[d, k], recv_sem=rs_recv.at[d, k],
            device_id={"gx": px, "yz": py}, device_id_type=MESH,
        )

    mine = pl.ds(pl.multiple_of(me * chunk, chunk), chunk)

    def gather(d, k):
        px, py = peer(k)
        return pltpu.make_async_remote_copy(
            src_ref=out_ref.at[d, mine],
            dst_ref=out_ref.at[d, mine],
            send_sem=ag_send.at[d, k], recv_sem=ag_recv.at[d, k],
            device_id={"gx": px, "yz": py}, device_id_type=MESH,
        )

    def reduce_and_gather(d):
        total = part[d, mine]
        for k in range(1, ranks):
            scatter(d, k).wait_recv()
            total = total + landed[d, k]
        out_ref[d, mine] = total * scaling
        for k in range(1, ranks):
            gather(d, k).start()

    acc[...] = jnp.zeros_like(acc)
    gauge_copy(0).wait()
    row_copy(0).wait()

    @pl.loop(0, nx)
    def _(x):
        @pl.when(x < nx - 1)
        def _():
            row_copy(x + 1).wait()

        @pl.when(x == nx - 1)
        def _():
            halo_x.wait_recv()

        turned = left([(x, y) for y in range(ny)]).T
        vt[x] = turned
        found = links(0, x)
        images = [image(found, y, v[:, :, x + 1, y]) for y in range(ny)]
        acc[...] += jnp.dot(
            turned, jnp.concatenate(images, 0), preferred_element_type=jnp.float32
        )

    finish(0)
    for k in range(1, ranks):
        scatter(0, k).start()

    acc[...] = jnp.zeros_like(acc)
    gauge_copy(1).wait()

    @pl.loop(0, nx)
    def _(x):
        found = links(1, x)
        images = [image(found, y, v[:, :, x, y + 1]) for y in range(ny - 1)]
        images.append(jnp.zeros((rows, 2 * nv), jnp.bfloat16))
        acc[...] += jnp.dot(
            vt[x], jnp.concatenate(images, 0), preferred_element_type=jnp.float32
        )

    reduce_and_gather(0)
    halo_y.wait_recv()
    images = [image(links(1, x), ny - 1, hy[:, :, x]) for x in range(nx)]
    acc[...] += jnp.dot(
        left([(x, ny - 1) for x in range(nx)]).T, jnp.concatenate(images, 0),
        preferred_element_type=jnp.float32,
    )
    finish(1)
    for k in range(1, ranks):
        scatter(1, k).start()
    reduce_and_gather(1)

    for d in range(2):
        for k in range(1, ranks):
            gather(d, k).wait_recv()
    halo_x.wait_send()
    halo_y.wait_send()
    for d in range(2):
        for k in range(1, ranks):
            scatter(d, k).wait_send()
            gather(d, k).wait_send()


def local(vectors, gauge_x, gauge_y):
    ngx, nyz = lax.axis_size("gx"), lax.axis_size("yz")
    _, _, nx, ny, nz, nv = vectors.shape
    ranks = ngx * nyz
    scaling = 1.0 / math.sqrt(3.0 * nx * ngx * ny * nyz * nz)
    sites = 3 * nx * ny * nz
    out = pl.pallas_call(
        functools.partial(kernel, ngx, nyz, scaling),
        out_shape=jax.ShapeDtypeStruct((2, 2 * nv, nv), jnp.float32),
        in_specs=[pl.BlockSpec(memory_space=pl.ANY)] * 3,
        out_specs=pl.BlockSpec(memory_space=pltpu.VMEM),
        scratch_shapes=[
            pltpu.VMEM((2, 3, nx + 1, ny, nz, nv), jnp.bfloat16),
            pltpu.VMEM((2, 3, nx, nz, nv), jnp.bfloat16),
            pltpu.VMEM((2,) + gauge_x.shape, jnp.float32),
            pltpu.VMEM((nx, 2 * nv, 3 * ny * nz), jnp.bfloat16),
            pltpu.VMEM((2 * nv, 2 * nv), jnp.float32),
            pltpu.VMEM((2, 2 * nv, nv), jnp.float32),
            pltpu.VMEM((2, ranks, 2 * nv // ranks, nv), jnp.float32),
            pltpu.SemaphoreType.DMA((nx,)),
            pltpu.SemaphoreType.DMA((2,)),
            pltpu.SemaphoreType.DMA((2,)),
            pltpu.SemaphoreType.DMA((2,)),
            pltpu.SemaphoreType.DMA((2, ranks)),
            pltpu.SemaphoreType.DMA((2, ranks)),
            pltpu.SemaphoreType.DMA((2, ranks)),
            pltpu.SemaphoreType.DMA((2, ranks)),
        ],
        compiler_params=pltpu.CompilerParams(
            collective_id=0, has_side_effects=True, vmem_limit_bytes=32 * 1024 * 1024
        ),
        cost_estimate=pl.CostEstimate(
            flops=24 * sites * nv * nv, bytes_accessed=4 * sites * nv, transcendentals=0
        ),
        name="elementals",
    )(vectors, gauge_x, gauge_y)
    return out.reshape(2, 2, nv, nv)


def solution(mesh):
    placed = (
        P(None, None, "gx", "yz", "ta", None),
        P(None, None, None, "gx", "yz", "ta"),
        P(None, None, None, "gx", "yz", "ta"),
    )
    return jax.shard_map(
        local, mesh=mesh, in_specs=placed, out_specs=P("ta", None, None, None), check_vma=False
    )
```

time: 137 us -> 38.5 us (0.28)
  waiting for transfers between devices: 89.4 us -> 0 us
  Pallas kernels: 0 us -> 33.5 us
  other arithmetic: 18.8 us -> 0 us
  between operations: 13.6 us -> 0.01 us
  starting transfers between devices: 6.09 us -> 0 us
  matrix products: 4.18 us -> 0 us
    psum x1 -> x0, waiting for transfers between devices: 89.4 us -> none  [local(): lax.psum(jnp.concatenate([contract(left_rows, member) for member in block...]
    pallas_call x0 -> x1, Pallas kernels: none -> 33.5 us  [local(): pl.pallas_call(functools.partial(kernel, ngx, nyz, scaling), out_shape=ja...]
    another operation x8 -> x0, other arithmetic: 16.5 us -> none
    ppermute x2 -> x0, starting transfers between devices: 6.08 us -> none  [shifted(): return lax.ppermute(value, axis, pairs)]
    unnamed x6 -> x7, local copies, waits for them, and re-layouts: 0.49 us -> 4.72 us
    dot_general x4 -> x0, matrix products: 4.18 us -> none  [contract(): lax.dot_general(left_cols, right_cols, (((0,), (0,)), ((), ())), preferre...]
    slice x5 -> x0, local copies, waits for them, and re-layouts: 3.59 us -> none  [the longest x1 1.03 us: local(): from_next_y = shifted(vectors[:, :, :, :1], 'yz', -1)]
  transfers between devices with their start and end apart: 3 -> 0, of which waited for: 1 -> 0; matrix products, arithmetic and copies ran while one was open for 9% -> 0% of each run, Pallas kernels for 0% -> 0%
where the time goes in v1:
time: 38.5 us; the launch traced here: 38.2 us
  Pallas kernels  33.5 us (87%)
  local copies, waits for them, and re-layouts  4.72 us (12%)
    pallas_call x1, Pallas kernels, local(): pl.pallas_call(functools.partial(kernel, ngx, nyz, scaling), out_shape=ja...  33.5 us
    unnamed x7, local copies, waits for them, and re-layouts  4.72 us

profile of v1, /device:TPU:0, one launch (start us, length us, event | category | flops | bytes accessed | tf_op | source)
XLA Modules:
  0.0 38.2 jit_solution(15394201572079533033)
XLA Ops:
  0.0 0.0 copy-start
  0.0 1.9 %copy-done = bf16[2,3,8,8,32,128]{5,4,3,2,1,0:T(8,128)(2,1)S(1)} copy-done((bf16[2,3,8,8,32,128]{5,4,3,2,1,0:T(8,128)(2,1)S(1)}, bf16[2,3,8,8,32,128]{5,4,3,2,1,0:T(8,128)(2,1)}, u32[]{:S(2)}) %copy-start) | copy-done | bytes 3145752
  1.9 0.0 copy-start.1
  1.9 1.1 %copy-done.1 = f32[2,3,3,8,8,32]{5,4,3,2,1,0:T(8,128)S(1)} copy-done((f32[2,3,3,8,8,32]{5,4,3,2,1,0:T(8,128)S(1)}, f32[2,3,3,8,8,32]{5,4,3,2,1,0:T(8,128)}, u32[]{:S(2)}) %copy-start.1) | copy-done | bytes 147480
  3.0 0.0 copy-start.2
  3.0 1.1 %copy-done.2 = f32[2,3,3,8,8,32]{5,4,3,2,1,0:T(8,128)S(1)} copy-done((f32[2,3,3,8,8,32]{5,4,3,2,1,0:T(8,128)S(1)}, f32[2,3,3,8,8,32]{5,4,3,2,1,0:T(8,128)}, u32[]{:S(2)}) %copy-start.2) | copy-done | bytes 147480
  4.0 33.5 %elementals.1 = f32[2,256,128]{2,1,0:T(8,128)S(1)} custom-call(bf16[2,3,8,8,32,128]{5,4,3,2,1,0:T(8,128)(2,1)S(1)} %copy-done, f32[2,3,3,8,8,32]{5,4,3,2,1,0:T(8,128)S(1)} %copy-done.1, f32[2,3,3,8,8,32]{5,4,3,2,1,0:T(8,128)S(1)} %copy-done.2), custom_call_target="tpu_custom_call" | custom-call | flops 2415919104 | bytes 3145728 | tf_op jit(solution)/shard_map/elementals/pallas_call | solution.py:204
  37.5 0.7 %copy.5 = f32[2,2,128,128]{3,2,1,0:T(8,128)} copy(f32[2,2,128,128]{3,2,1,0:T(8,128)S(1)} %bitcast.1) | data formatting | bytes 524288
Async XLA Ops:
  0.0 1.9 %copy-start = (bf16[2,3,8,8,32,128]{5,4,3,2,1,0:T(8,128)(2,1)S(1)}, bf16[2,3,8,8,32,128]{5,4,3,2,1,0:T(8,128)(2,1)}, u32[]{:S(2)}) copy-start(bf16[2,3,8,8,32,128]{5,4,3,2,1,0:T(8,128)(2,1)} %v_hbm.1) | copy-start | bytes 9437188
  1.9 1.1 %copy-start.1 = (f32[2,3,3,8,8,32]{5,4,3,2,1,0:T(8,128)S(1)}, f32[2,3,3,8,8,32]{5,4,3,2,1,0:T(8,128)}, u32[]{:S(2)}) copy-start(f32[2,3,3,8,8,32]{5,4,3,2,1,0:T(8,128)} %gx_hbm.1) | copy-start | bytes 442372
  3.0 1.1 %copy-start.2 = (f32[2,3,3,8,8,32]{5,4,3,2,1,0:T(8,128)S(1)}, f32[2,3,3,8,8,32]{5,4,3,2,1,0:T(8,128)}, u32[]{:S(2)}) copy-start(f32[2,3,3,8,8,32]{5,4,3,2,1,0:T(8,128)} %gy_hbm.1) | copy-start | bytes 442372

commit v2 on v1

--- a/solution.py
+++ b/solution.py
@@ -14,16 +14,19 @@
 def kernel(
     ngx, nyz, scaling,
     v_hbm, gx_hbm, gy_hbm, out_ref,
-    v, hy, gauge, vt, acc, part, landed,
-    load_sem, gauge_sem, halo_send, halo_recv, rs_send, rs_recv, ag_send, ag_recv,
+    v, hy, gauge, vt, acc, part, swapped, landed,
+    load_sem, gauge_sem, halo_send, halo_recv, swap_send, swap_recv,
+    rs_send, rs_recv, ag_send, ag_recv, fw_send, fw_recv,
 ):
     nx, ny, nz, nv = v_hbm.shape[2:]
     rows = 3 * nz
-    ranks = ngx * nyz
-    chunk = 2 * nv // ranks
+    half_gx = ngx // 2
+    chips = half_gx * nyz
+    chunk = nv // chips
     my_x = lax.axis_index("gx")
     my_y = lax.axis_index("yz")
-    me = my_x * nyz + my_y
+    core = lax.rem(my_x, 2)
+    me = (my_x // 2) * nyz + my_y
 
     def gauge_copy(d):
         return pltpu.make_async_copy((gx_hbm, gy_hbm)[d], gauge.at[d], gauge_sem.at[d])
@@ -38,15 +41,20 @@
 
     def peer(k):
         kx, ky = k // nyz, k % nyz
-        return lax.rem(my_x + kx, ngx), lax.rem(my_y + ky, nyz)
+        return lax.rem(my_x + 2 * kx, ngx), lax.rem(my_y + ky, nyz)
 
     barrier = pltpu.get_barrier_semaphore()
-    for k in range(1, ranks):
-        px, py = peer(k)
-        pl.semaphore_signal(
-            barrier, inc=1, device_id={"gx": px, "yz": py}, device_id_type=MESH
-        )
-    pl.semaphore_wait(barrier, ranks - 1)
+    for kx in range(ngx):
+        for ky in range(nyz):
+            if (kx, ky) != (0, 0):
+                pl.semaphore_signal(
+                    barrier, inc=1,
+                    device_id={
+                        "gx": lax.rem(my_x + kx, ngx), "yz": lax.rem(my_y + ky, nyz)
+                    },
+                    device_id_type=MESH,
+                )
+    pl.semaphore_wait(barrier, ngx * nyz - 1)
 
     halo_x = pltpu.make_async_remote_copy(
         src_ref=v_hbm.at[:, :, 0], dst_ref=v.at[:, :, nx],
@@ -104,35 +112,67 @@
         part[d, :nv] = total[:nv, :nv] + total[nv:, nv:]
         part[d, nv:] = total[:nv, nv:] - total[nv:, :nv]
 
+    sibling = {"gx": my_x + 1 - 2 * core}
+    half = pl.ds(pl.multiple_of(core * nv, nv), nv)
+    other_half = pl.ds(pl.multiple_of((1 - core) * nv, nv), nv)
+
+    def chunk_of(owner):
+        return pl.ds(pl.multiple_of(core * nv + owner * chunk, chunk), chunk)
+
+    def swap(d):
+        return pltpu.make_async_remote_copy(
+            src_ref=part.at[d, other_half], dst_ref=swapped.at[d],
+            send_sem=swap_send.at[d], recv_sem=swap_recv.at[d],
+            device_id=sibling, device_id_type=MESH,
+        )
+
     def scatter(d, k):
         px, py = peer(k)
-        owner = px * nyz + py
-        return pltpu.make_async_remote_copy(
-            src_ref=part.at[d, pl.ds(pl.multiple_of(owner * chunk, chunk), chunk)],
-            dst_ref=landed.at[d, k],
+        owner = (px // 2) * nyz + py
+        return pltpu.make_async_remote_copy(
+            src_ref=part.at[d, chunk_of(owner)], dst_ref=landed.at[d, k],
             send_sem=rs_send.at[d, k], recv_sem=rs_recv.at[d, k],
             device_id={"gx": px, "yz": py}, device_id_type=MESH,
         )
 
-    mine = pl.ds(pl.multiple_of(me * chunk, chunk), chunk)
-
     def gather(d, k):
         px, py = peer(k)
         return pltpu.make_async_remote_copy(
-            src_ref=out_ref.at[d, mine],
-            dst_ref=out_ref.at[d, mine],
+            src_ref=out_ref.at[d, chunk_of(me)], dst_ref=out_ref.at[d, chunk_of(me)],
             send_sem=ag_send.at[d, k], recv_sem=ag_recv.at[d, k],
             device_id={"gx": px, "yz": py}, device_id_type=MESH,
         )
 
+    def forward(d, k):
+        fx = lax.rem(my_x // 2 + half_gx - k // nyz, half_gx)
+        fy = lax.rem(my_y + nyz - k % nyz, nyz)
+        rows_k = chunk_of(fx * nyz + fy)
+        return pltpu.make_async_remote_copy(
+            src_ref=out_ref.at[d, rows_k], dst_ref=out_ref.at[d, rows_k],
+            send_sem=fw_send.at[d, k], recv_sem=fw_recv.at[d, k],
+            device_id=sibling, device_id_type=MESH,
+        )
+
+    def start_scatter(d):
+        swap(d).wait_recv()
+        part[d, half] = part[d, half] + swapped[d]
+        for k in range(1, chips):
+            scatter(d, k).start()
+
     def reduce_and_gather(d):
-        total = part[d, mine]
-        for k in range(1, ranks):
+        total = part[d, chunk_of(me)]
+        for k in range(1, chips):
             scatter(d, k).wait_recv()
             total = total + landed[d, k]
-        out_ref[d, mine] = total * scaling
-        for k in range(1, ranks):
+        out_ref[d, chunk_of(me)] = total * scaling
+        for k in range(1, chips):
             gather(d, k).start()
+        forward(d, 0).start()
+
+    def pass_on(d):
+        for k in range(1, chips):
+            gather(d, k).wait_recv()
+            forward(d, k).start()
 
     acc[...] = jnp.zeros_like(acc)
     gauge_copy(0).wait()
@@ -157,14 +197,17 @@
         )
 
     finish(0)
-    for k in range(1, ranks):
-        scatter(0, k).start()
+    swap(0).start()
 
     acc[...] = jnp.zeros_like(acc)
     gauge_copy(1).wait()
 
     @pl.loop(0, nx)
     def _(x):
+        @pl.when(x == 2)
+        def _():
+            start_scatter(0)
+
         found = links(1, x)
         images = [image(found, y, v[:, :, x, y + 1]) for y in range(ny - 1)]
         images.append(jnp.zeros((rows, 2 * nv), jnp.bfloat16))
@@ -180,25 +223,30 @@
         preferred_element_type=jnp.float32,
     )
     finish(1)
-    for k in range(1, ranks):
-        scatter(1, k).start()
+    swap(1).start()
+    pass_on(0)
+    start_scatter(1)
     reduce_and_gather(1)
+    pass_on(1)
 
     for d in range(2):
-        for k in range(1, ranks):
-            gather(d, k).wait_recv()
+        for k in range(chips):
+            forward(d, k).wait_recv()
     halo_x.wait_send()
     halo_y.wait_send()
     for d in range(2):
-        for k in range(1, ranks):
-            scatter(d, k).wait_send()
-            gather(d, k).wait_send()
+        swap(d).wait_send()
+        for k in range(chips):
+            forward(d, k).wait_send()
+            if k > 0:
+                scatter(d, k).wait_send()
+                gather(d, k).wait_send()
 
 
 def local(vectors, gauge_x, gauge_y):
     ngx, nyz = lax.axis_size("gx"), lax.axis_size("yz")
     _, _, nx, ny, nz, nv = vectors.shape
-    ranks = ngx * nyz
+    chips = ngx // 2 * nyz
     scaling = 1.0 / math.sqrt(3.0 * nx * ngx * ny * nyz * nz)
     sites = 3 * nx * ny * nz
     out = pl.pallas_call(
@@ -213,18 +261,23 @@
             pltpu.VMEM((nx, 2 * nv, 3 * ny * nz), jnp.bfloat16),
             pltpu.VMEM((2 * nv, 2 * nv), jnp.float32),
             pltpu.VMEM((2, 2 * nv, nv), jnp.float32),
-            pltpu.VMEM((2, ranks, 2 * nv // ranks, nv), jnp.float32),
+            pltpu.VMEM((2, nv, nv), jnp.float32),
+            pltpu.VMEM((2, chips, nv // chips, nv), jnp.float32),
             pltpu.SemaphoreType.DMA((nx,)),
             pltpu.SemaphoreType.DMA((2,)),
             pltpu.SemaphoreType.DMA((2,)),
             pltpu.SemaphoreType.DMA((2,)),
-            pltpu.SemaphoreType.DMA((2, ranks)),
-            pltpu.SemaphoreType.DMA((2, ranks)),
-            pltpu.SemaphoreType.DMA((2, ranks)),
-            pltpu.SemaphoreType.DMA((2, ranks)),
+            pltpu.SemaphoreType.DMA((2,)),
+            pltpu.SemaphoreType.DMA((2,)),
+            pltpu.SemaphoreType.DMA((2, chips)),
+            pltpu.SemaphoreType.DMA((2, chips)),
+            pltpu.SemaphoreType.DMA((2, chips)),
+            pltpu.SemaphoreType.DMA((2, chips)),
+            pltpu.SemaphoreType.DMA((2, chips)),
+            pltpu.SemaphoreType.DMA((2, chips)),
         ],
         compiler_params=pltpu.CompilerParams(
-            collective_id=0, has_side_effects=True, vmem_limit_bytes=32 * 1024 * 1024
+            collective_id=0, has_side_effects=True, vmem_limit_bytes=63 * 1024 * 1024
         ),
         cost_estimate=pl.CostEstimate(
             flops=24 * sites * nv * nv, bytes_accessed=4 * sites * nv, transcendentals=0

time: 38.5 us -> 36.8 us (0.956)
  local copies, waits for them, and re-layouts: 4.72 us -> 1.67 us
  Pallas kernels: 33.5 us -> 35 us
    unnamed x7 -> x1, local copies, waits for them, and re-layouts: 4.72 us -> 1.67 us
    pallas_call x1, Pallas kernels: 33.5 us -> 35 us  [local(): pl.pallas_call(functools.partial(kernel, ngx, nyz, scaling), out_shape=ja...]
where the time goes in v2:
time: 36.8 us; the launch traced here: 36.7 us
  Pallas kernels  35 us (95%)
  local copies, waits for them, and re-layouts  1.67 us (5%)
    pallas_call x1, Pallas kernels, local(): pl.pallas_call(functools.partial(kernel, ngx, nyz, scaling), out_shape=ja...  35 us
    unnamed x1, local copies, waits for them, and re-layouts  1.67 us

profile of v2, /device:TPU:0, one launch (start us, length us, event | category | flops | bytes accessed | tf_op | source)
XLA Modules:
  0.0 36.7 jit_solution(16273838952036289881)
XLA Ops:
  0.0 35.0 %elementals.1 = f32[2,256,128]{2,1,0:T(8,128)} custom-call(bf16[2,3,8,8,32,128]{5,4,3,2,1,0:T(8,128)(2,1)} %v_hbm.1, f32[2,3,3,8,8,32]{5,4,3,2,1,0:T(8,128)} %gx_hbm.1, f32[2,3,3,8,8,32]{5,4,3,2,1,0:T(8,128)} %gy_hbm.1), custom_call_target="tpu_custom_call" | custom-call | flops 2415919104 | bytes 3145728 | tf_op jit(solution)/shard_map/elementals/pallas_call | solution.py:252
  35.0 1.7 %copy.5 = f32[2,2,128,128]{3,2,1,0:T(8,128)} copy(f32[2,2,128,128]{3,2,1,0:T(8,128)} %bitcast.1) | data formatting | bytes 524288

commit v3 on v2

--- a/solution.py
+++ b/solution.py
@@ -9,10 +9,12 @@
 from jax.sharding import PartitionSpec as P
 
 MESH = pl.DeviceIdType.MESH
+GROUP_X = 2
+GROUP_Y = 4
 
 
 def kernel(
-    ngx, nyz, scaling,
+    ngx, nyz,
     v_hbm, gx_hbm, gy_hbm, out_ref,
     v, hy, gauge, vt, acc, part, swapped, landed,
     load_sem, gauge_sem, halo_send, halo_recv, swap_send, swap_recv,
@@ -54,7 +56,6 @@
                     },
                     device_id_type=MESH,
                 )
-    pl.semaphore_wait(barrier, ngx * nyz - 1)
 
     halo_x = pltpu.make_async_remote_copy(
         src_ref=v_hbm.at[:, :, 0], dst_ref=v.at[:, :, nx],
@@ -66,9 +67,6 @@
         send_sem=halo_send.at[1], recv_sem=halo_recv.at[1],
         device_id={"yz": lax.rem(my_y + nyz - 1, nyz)}, device_id_type=MESH,
     )
-    halo_x.start()
-    halo_y.start()
-
     lanes = lax.broadcasted_iota(jnp.int32, (nz, 2 * rows), 1) % nz
     subs = lax.broadcasted_iota(jnp.int32, (nz, 2 * rows), 0)
     diagonal = jnp.where(lanes == subs, 1.0, 0.0).astype(jnp.bfloat16)
@@ -164,7 +162,7 @@
         for k in range(1, chips):
             scatter(d, k).wait_recv()
             total = total + landed[d, k]
-        out_ref[d, chunk_of(me)] = total * scaling
+        out_ref[d, chunk_of(me)] = total
         for k in range(1, chips):
             gather(d, k).start()
         forward(d, 0).start()
@@ -178,23 +176,39 @@
     gauge_copy(0).wait()
     row_copy(0).wait()
 
-    @pl.loop(0, nx)
-    def _(x):
-        @pl.when(x < nx - 1)
+    def rows_x(first):
+        for x in [first + i for i in range(GROUP_X)]:
+            turned = left([(x, y) for y in range(ny)]).T
+            vt[x] = turned
+            found = links(0, x)
+            images = [image(found, y, v[:, :, x + 1, y]) for y in range(ny)]
+            acc[...] += jnp.dot(
+                turned, jnp.concatenate(images, 0), preferred_element_type=jnp.float32
+            )
+
+    for x in range(1, GROUP_X + 1):
+        row_copy(x).wait()
+    rows_x(0)
+
+    pl.semaphore_wait(barrier, ngx * nyz - 1)
+    halo_x.start()
+    halo_y.start()
+
+    @pl.loop(1, nx // GROUP_X)
+    def _(group):
+        first = group * GROUP_X
+        for i in range(1, GROUP_X):
+            row_copy(first + i).wait()
+
+        @pl.when(group < nx // GROUP_X - 1)
         def _():
-            row_copy(x + 1).wait()
-
-        @pl.when(x == nx - 1)
+            row_copy(first + GROUP_X).wait()
+
+        @pl.when(group == nx // GROUP_X - 1)
         def _():
             halo_x.wait_recv()
 
-        turned = left([(x, y) for y in range(ny)]).T
-        vt[x] = turned
-        found = links(0, x)
-        images = [image(found, y, v[:, :, x + 1, y]) for y in range(ny)]
-        acc[...] += jnp.dot(
-            turned, jnp.concatenate(images, 0), preferred_element_type=jnp.float32
-        )
+        rows_x(first)
 
     finish(0)
     swap(0).start()
@@ -202,18 +216,19 @@
     acc[...] = jnp.zeros_like(acc)
     gauge_copy(1).wait()
 
-    @pl.loop(0, nx)
-    def _(x):
-        @pl.when(x == 2)
+    @pl.loop(0, nx // GROUP_Y)
+    def _(group):
+        @pl.when(group == 1)
         def _():
             start_scatter(0)
 
-        found = links(1, x)
-        images = [image(found, y, v[:, :, x, y + 1]) for y in range(ny - 1)]
-        images.append(jnp.zeros((rows, 2 * nv), jnp.bfloat16))
-        acc[...] += jnp.dot(
-            vt[x], jnp.concatenate(images, 0), preferred_element_type=jnp.float32
-        )
+        for x in [group * GROUP_Y + i for i in range(GROUP_Y)]:
+            found = links(1, x)
+            images = [image(found, y, v[:, :, x, y + 1]) for y in range(ny - 1)]
+            images.append(jnp.zeros((rows, 2 * nv), jnp.bfloat16))
+            acc[...] += jnp.dot(
+                vt[x], jnp.concatenate(images, 0), preferred_element_type=jnp.float32
+            )
 
     reduce_and_gather(0)
     halo_y.wait_recv()
@@ -250,7 +265,7 @@
     scaling = 1.0 / math.sqrt(3.0 * nx * ngx * ny * nyz * nz)
     sites = 3 * nx * ny * nz
     out = pl.pallas_call(
-        functools.partial(kernel, ngx, nyz, scaling),
+        functools.partial(kernel, ngx, nyz),
         out_shape=jax.ShapeDtypeStruct((2, 2 * nv, nv), jnp.float32),
         in_specs=[pl.BlockSpec(memory_space=pl.ANY)] * 3,
         out_specs=pl.BlockSpec(memory_space=pltpu.VMEM),
@@ -284,7 +299,7 @@
         ),
         name="elementals",
     )(vectors, gauge_x, gauge_y)
-    return out.reshape(2, 2, nv, nv)
+    return (out * scaling).reshape(2, 2, nv, nv)
 
 
 def solution(mesh):

time: 36.8 us -> 36.8 us (level)
  other arithmetic: 0 us -> 1.68 us
  local copies, waits for them, and re-layouts: 1.67 us -> 0 us
    mul x0 -> x1, other arithmetic: none -> 1.68 us  [local(): return (out * scaling).reshape(2, 2, nv, nv)]
    unnamed x1 -> x0, local copies, waits for them, and re-layouts: 1.67 us -> none
where the time goes in v3:
time: 36.8 us; the launch traced here: 36.6 us
  Pallas kernels  35 us (95%)
  other arithmetic  1.68 us (5%)
    pallas_call x1, Pallas kernels, local(): pl.pallas_call(functools.partial(kernel, ngx, nyz), out_shape=jax.ShapeDt...  35 us
    mul x1, other arithmetic, local(): return (out * scaling).reshape(2, 2, nv, nv)  1.68 us

profile of v3, /device:TPU:0, one launch (start us, length us, event | category | flops | bytes accessed | tf_op | source)
XLA Modules:
  0.0 36.6 jit_solution(3152933119933134309)
XLA Ops:
  0.0 35.0 %elementals.1 = f32[2,256,128]{2,1,0:T(8,128)} custom-call(bf16[2,3,8,8,32,128]{5,4,3,2,1,0:T(8,128)(2,1)} %v_hbm.1, f32[2,3,3,8,8,32]{5,4,3,2,1,0:T(8,128)} %gx_hbm.1, f32[2,3,3,8,8,32]{5,4,3,2,1,0:T(8,128)} %gy_hbm.1), custom_call_target="tpu_custom_call" | custom-call | flops 2415919104 | bytes 3145728 | tf_op jit(solution)/shard_map/elementals/pallas_call | solution.py:267
  35.0 1.7 %broadcast_multiply_fusion = f32[2,256,128]{2,1,0:T(8,128)} fusion(f32[2,256,128]{2,1,0:T(8,128)} %elementals.1), kind=kLoop, calls=%fused_computation | loop fusion | flops 65536 | bytes 524288 | tf_op jit(solution)/shard_map/mul | solution.py:302

commit v4 on v3

--- a/solution.py
+++ b/solution.py
@@ -9,8 +9,8 @@
 from jax.sharding import PartitionSpec as P
 
 MESH = pl.DeviceIdType.MESH
-GROUP_X = 2
-GROUP_Y = 4
+GROUP_X = 1
+GROUP_Y = 1
 
 
 def kernel(
@@ -67,34 +67,29 @@
         send_sem=halo_send.at[1], recv_sem=halo_recv.at[1],
         device_id={"yz": lax.rem(my_y + nyz - 1, nyz)}, device_id_type=MESH,
     )
-    lanes = lax.broadcasted_iota(jnp.int32, (nz, 2 * rows), 1) % nz
-    subs = lax.broadcasted_iota(jnp.int32, (nz, 2 * rows), 0)
-    diagonal = jnp.where(lanes == subs, 1.0, 0.0).astype(jnp.bfloat16)
-
     def links(d, x):
-        found = []
+        return gauge[d, :, :, :, x].reshape(18 * ny, nz).T
+
+    def image(columns, y, source):
+        def link(r, a, b):
+            at = ((r * 3 + a) * 3 + b) * ny + y
+            return columns[:, at : at + 1]
+
+        wide = source.astype(jnp.float32)
+        real_parts, imag_parts = [], []
         for a in range(3):
-            pieces = [gauge[d, r, a, b, x] for r in range(2) for b in range(3)]
-            full = jnp.concatenate(pieces, axis=1)
-            high = full.astype(jnp.bfloat16).astype(jnp.float32)
-            found.append((high, full - high))
-        return found
-
-    def spread(row):
-        wide = jnp.broadcast_to(row, (nz, 2 * rows)).astype(jnp.bfloat16)
-        return wide * diagonal
-
-    def image(found, y, source):
-        real = source[0].reshape(rows, nv)
-        imag = source[1].reshape(rows, nv)
-        weights = jnp.concatenate(
-            [jnp.concatenate([real, -imag], 0), jnp.concatenate([imag, real], 0)], 1
-        )
-        parts = [spread(found[a][p][y : y + 1]) for p in range(2) for a in range(3)]
-        both = jnp.dot(
-            jnp.concatenate(parts, 0), weights, preferred_element_type=jnp.float32
-        )
-        return (both[:rows] + both[rows:]).astype(jnp.bfloat16)
+            real, imag = None, None
+            for b in range(3):
+                lr, li = link(0, a, b), link(1, a, b)
+                r = lr * wide[0, b] - li * wide[1, b]
+                i = lr * wide[1, b] + li * wide[0, b]
+                real = r if real is None else real + r
+                imag = i if imag is None else imag + i
+            real_parts.append(real.astype(jnp.bfloat16))
+            imag_parts.append(imag.astype(jnp.bfloat16))
+        return jnp.concatenate(
+            [jnp.concatenate(real_parts, 0), jnp.concatenate(imag_parts, 0)], 1
+        )
 
     def left(sites):
         return jnp.concatenate(
@@ -218,7 +213,7 @@
 
     @pl.loop(0, nx // GROUP_Y)
     def _(group):
-        @pl.when(group == 1)
+        @pl.when(group == 2 // GROUP_Y)
         def _():
             start_scatter(0)
 

time: 36.8 us -> 42.3 us (1.15)
  Pallas kernels: 35 us -> 40.5 us
    pallas_call x1, Pallas kernels: 35 us -> 40.5 us  [local(): pl.pallas_call(functools.partial(kernel, ngx, nyz), out_shape=jax.ShapeDt...]
where the time goes in v4:
time: 42.3 us; the launch traced here: 42.2 us
  Pallas kernels  40.5 us (96%)
  other arithmetic  1.68 us (4%)
    pallas_call x1, Pallas kernels, local(): pl.pallas_call(functools.partial(kernel, ngx, nyz), out_shape=jax.ShapeDt...  40.5 us
    mul x1, other arithmetic, local(): return (out * scaling).reshape(2, 2, nv, nv)  1.68 us

profile of v4, /device:TPU:0, one launch (start us, length us, event | category | flops | bytes accessed | tf_op | source)
XLA Modules:
  0.0 42.2 jit_solution(4593781387304262956)
XLA Ops:
  0.0 40.5 %elementals.1 = f32[2,256,128]{2,1,0:T(8,128)} custom-call(bf16[2,3,8,8,32,128]{5,4,3,2,1,0:T(8,128)(2,1)} %v_hbm.1, f32[2,3,3,8,8,32]{5,4,3,2,1,0:T(8,128)} %gx_hbm.1, f32[2,3,3,8,8,32]{5,4,3,2,1,0:T(8,128)} %gy_hbm.1), custom_call_target="tpu_custom_call" | custom-call | flops 2415919104 | bytes 3145728 | tf_op jit(solution)/shard_map/elementals/pallas_call | solution.py:262
  40.5 1.7 %broadcast_multiply_fusion = f32[2,256,128]{2,1,0:T(8,128)} fusion(f32[2,256,128]{2,1,0:T(8,128)} %elementals.1), kind=kLoop, calls=%fused_computation | loop fusion | flops 65536 | bytes 524288 | tf_op jit(solution)/shard_map/mul | solution.py:297

commit v5 on v4

--- a/solution.py
+++ b/solution.py
@@ -67,10 +67,39 @@
         send_sem=halo_send.at[1], recv_sem=halo_recv.at[1],
         device_id={"yz": lax.rem(my_y + nyz - 1, nyz)}, device_id_type=MESH,
     )
+    lanes = lax.broadcasted_iota(jnp.int32, (nz, 2 * rows), 1) % nz
+    subs = lax.broadcasted_iota(jnp.int32, (nz, 2 * rows), 0)
+    diagonal = jnp.where(lanes == subs, 1.0, 0.0).astype(jnp.bfloat16)
+
+    def link_rows(d, x):
+        found = []
+        for a in range(3):
+            pieces = [gauge[d, r, a, b, x] for r in range(2) for b in range(3)]
+            full = jnp.concatenate(pieces, axis=1)
+            high = full.astype(jnp.bfloat16).astype(jnp.float32)
+            found.append((high, full - high))
+        return found
+
+    def spread(row):
+        wide = jnp.broadcast_to(row, (nz, 2 * rows)).astype(jnp.bfloat16)
+        return wide * diagonal
+
+    def image_by_matmul(found, y, source):
+        real = source[0].reshape(rows, nv)
+        imag = source[1].reshape(rows, nv)
+        weights = jnp.concatenate(
+            [jnp.concatenate([real, -imag], 0), jnp.concatenate([imag, real], 0)], 1
+        )
+        parts = [spread(found[a][p][y : y + 1]) for p in range(2) for a in range(3)]
+        both = jnp.dot(
+            jnp.concatenate(parts, 0), weights, preferred_element_type=jnp.float32
+        )
+        return (both[:rows] + both[rows:]).astype(jnp.bfloat16)
+
     def links(d, x):
         return gauge[d, :, :, :, x].reshape(18 * ny, nz).T
 
-    def image(columns, y, source):
+    def image_by_products(columns, y, source):
         def link(r, a, b):
             at = ((r * 3 + a) * 3 + b) * ny + y
             return columns[:, at : at + 1]
@@ -91,6 +120,16 @@
             [jnp.concatenate(real_parts, 0), jnp.concatenate(imag_parts, 0)], 1
         )
 
+    def row_images(d, x, count, source_of):
+        found, columns = link_rows(d, x), links(d, x)
+        images = []
+        for y in range(count):
+            if y % 2 == 0:
+                images.append(image_by_matmul(found, y, source_of(y)))
+            else:
+                images.append(image_by_products(columns, y, source_of(y)))
+        return images
+
     def left(sites):
         return jnp.concatenate(
             [
@@ -175,8 +214,7 @@
         for x in [first + i for i in range(GROUP_X)]:
             turned = left([(x, y) for y in range(ny)]).T
             vt[x] = turned
-            found = links(0, x)
-            images = [image(found, y, v[:, :, x + 1, y]) for y in range(ny)]
+            images = row_images(0, x, ny, lambda y: v[:, :, x + 1, y])
             acc[...] += jnp.dot(
                 turned, jnp.concatenate(images, 0), preferred_element_type=jnp.float32
             )
@@ -218,8 +256,7 @@
             start_scatter(0)
 
         for x in [group * GROUP_Y + i for i in range(GROUP_Y)]:
-            found = links(1, x)
-            images = [image(found, y, v[:, :, x, y + 1]) for y in range(ny - 1)]
+            images = row_images(1, x, ny - 1, lambda y: v[:, :, x, y + 1])
             images.append(jnp.zeros((rows, 2 * nv), jnp.bfloat16))
             acc[...] += jnp.dot(
                 vt[x], jnp.concatenate(images, 0), preferred_element_type=jnp.float32
@@ -227,7 +264,12 @@
 
     reduce_and_gather(0)
     halo_y.wait_recv()
-    images = [image(links(1, x), ny - 1, hy[:, :, x]) for x in range(nx)]
+    images = []
+    for x in range(nx):
+        if x % 2 == 0:
+            images.append(image_by_matmul(link_rows(1, x), ny - 1, hy[:, :, x]))
+        else:
+            images.append(image_by_products(links(1, x), ny - 1, hy[:, :, x]))
     acc[...] += jnp.dot(
         left([(x, ny - 1) for x in range(nx)]).T, jnp.concatenate(images, 0),
         preferred_element_type=jnp.float32,

time: 42.3 us -> 37.1 us (0.88)
  Pallas kernels: 40.5 us -> 35.3 us
    pallas_call x1, Pallas kernels: 40.5 us -> 35.3 us  [local(): pl.pallas_call(functools.partial(kernel, ngx, nyz), out_shape=jax.ShapeDt...]
where the time goes in v5:
time: 37.1 us; the launch traced here: 37 us
  Pallas kernels  35.3 us (95%)
  other arithmetic  1.68 us (5%)
    pallas_call x1, Pallas kernels, local(): pl.pallas_call(functools.partial(kernel, ngx, nyz), out_shape=jax.ShapeDt...  35.3 us
    mul x1, other arithmetic, local(): return (out * scaling).reshape(2, 2, nv, nv)  1.68 us

profile of v5, /device:TPU:0, one launch (start us, length us, event | category | flops | bytes accessed | tf_op | source)
XLA Modules:
  0.0 37.0 jit_solution(320163919498032906)
XLA Ops:
  0.0 35.3 %elementals.1 = f32[2,256,128]{2,1,0:T(8,128)} custom-call(bf16[2,3,8,8,32,128]{5,4,3,2,1,0:T(8,128)(2,1)} %v_hbm.1, f32[2,3,3,8,8,32]{5,4,3,2,1,0:T(8,128)} %gx_hbm.1, f32[2,3,3,8,8,32]{5,4,3,2,1,0:T(8,128)} %gy_hbm.1), custom_call_target="tpu_custom_call" | custom-call | flops 2415919104 | bytes 3145728 | tf_op jit(solution)/shard_map/elementals/pallas_call | solution.py:304
  35.3 1.7 %broadcast_multiply_fusion = f32[2,256,128]{2,1,0:T(8,128)} fusion(f32[2,256,128]{2,1,0:T(8,128)} %elementals.1), kind=kLoop, calls=%fused_computation | loop fusion | flops 65536 | bytes 524288 | tf_op jit(solution)/shard_map/mul | solution.py:339

commit v6 on v3

--- a/solution.py
+++ b/solution.py
@@ -14,7 +14,7 @@
 
 
 def kernel(
-    ngx, nyz,
+    ngx, nyz, scaling,
     v_hbm, gx_hbm, gy_hbm, out_ref,
     v, hy, gauge, vt, acc, part, swapped, landed,
     load_sem, gauge_sem, halo_send, halo_recv, swap_send, swap_recv,
@@ -57,6 +57,7 @@
                     device_id_type=MESH,
                 )
 
+    pl.semaphore_wait(barrier, ngx * nyz - 1)
     halo_x = pltpu.make_async_remote_copy(
         src_ref=v_hbm.at[:, :, 0], dst_ref=v.at[:, :, nx],
         send_sem=halo_send.at[0], recv_sem=halo_recv.at[0],
@@ -67,6 +68,9 @@
         send_sem=halo_send.at[1], recv_sem=halo_recv.at[1],
         device_id={"yz": lax.rem(my_y + nyz - 1, nyz)}, device_id_type=MESH,
     )
+    halo_x.start()
+    halo_y.start()
+
     lanes = lax.broadcasted_iota(jnp.int32, (nz, 2 * rows), 1) % nz
     subs = lax.broadcasted_iota(jnp.int32, (nz, 2 * rows), 0)
     diagonal = jnp.where(lanes == subs, 1.0, 0.0).astype(jnp.bfloat16)
@@ -162,7 +166,7 @@
         for k in range(1, chips):
             scatter(d, k).wait_recv()
             total = total + landed[d, k]
-        out_ref[d, chunk_of(me)] = total
+        out_ref[d, chunk_of(me)] = total * scaling
         for k in range(1, chips):
             gather(d, k).start()
         forward(d, 0).start()
@@ -190,9 +194,6 @@
         row_copy(x).wait()
     rows_x(0)
 
-    pl.semaphore_wait(barrier, ngx * nyz - 1)
-    halo_x.start()
-    halo_y.start()
 
     @pl.loop(1, nx // GROUP_X)
     def _(group):
@@ -265,7 +266,7 @@
     scaling = 1.0 / math.sqrt(3.0 * nx * ngx * ny * nyz * nz)
     sites = 3 * nx * ny * nz
     out = pl.pallas_call(
-        functools.partial(kernel, ngx, nyz),
+        functools.partial(kernel, ngx, nyz, scaling),
         out_shape=jax.ShapeDtypeStruct((2, 2 * nv, nv), jnp.float32),
         in_specs=[pl.BlockSpec(memory_space=pl.ANY)] * 3,
         out_specs=pl.BlockSpec(memory_space=pltpu.VMEM),
@@ -292,14 +293,14 @@
             pltpu.SemaphoreType.DMA((2, chips)),
         ],
         compiler_params=pltpu.CompilerParams(
-            collective_id=0, has_side_effects=True, vmem_limit_bytes=63 * 1024 * 1024
+            collective_id=0, has_side_effects=True, vmem_limit_bytes=int(53.3 * 1024 * 1024)
         ),
         cost_estimate=pl.CostEstimate(
             flops=24 * sites * nv * nv, bytes_accessed=4 * sites * nv, transcendentals=0
         ),
         name="elementals",
     )(vectors, gauge_x, gauge_y)
-    return (out * scaling).reshape(2, 2, nv, nv)
+    return out.reshape(2, 2, nv, nv)
 
 
 def solution(mesh):

time: 36.8 us -> 35.1 us (0.954)
  other arithmetic: 1.68 us -> 0 us
  local copies, waits for them, and re-layouts: 0 us -> 0.71 us
  Pallas kernels: 35 us -> 34.3 us
    mul x1 -> x0, other arithmetic: 1.68 us -> none  [local(): return (out * scaling).reshape(2, 2, nv, nv)]
    unnamed x0 -> x1, local copies, waits for them, and re-layouts: none -> 0.71 us
    pallas_call x1, Pallas kernels: 35 us -> 34.3 us  [local(): pl.pallas_call(functools.partial(kernel, ngx, nyz, scaling), out_shape=ja...]
where the time goes in v6:
time: 35.1 us; the launch traced here: 35 us
  Pallas kernels  34.3 us (98%)
  local copies, waits for them, and re-layouts  0.71 us (2%)
    pallas_call x1, Pallas kernels, local(): pl.pallas_call(functools.partial(kernel, ngx, nyz, scaling), out_shape=ja...  34.3 us
    unnamed x1, local copies, waits for them, and re-layouts  0.71 us

profile of v6, /device:TPU:0, one launch (start us, length us, event | category | flops | bytes accessed | tf_op | source)
XLA Modules:
  0.0 35.0 jit_solution(3178158004479353593)
XLA Ops:
  0.0 34.3 %elementals.1 = f32[2,256,128]{2,1,0:T(8,128)S(1)} custom-call(bf16[2,3,8,8,32,128]{5,4,3,2,1,0:T(8,128)(2,1)} %v_hbm.1, f32[2,3,3,8,8,32]{5,4,3,2,1,0:T(8,128)} %gx_hbm.1, f32[2,3,3,8,8,32]{5,4,3,2,1,0:T(8,128)} %gy_hbm.1), custom_call_target="tpu_custom_call" | custom-call | flops 2415919104 | bytes 3145728 | tf_op jit(solution)/shard_map/elementals/pallas_call | solution.py:268
  34.3 0.7 %copy.5 = f32[2,2,128,128]{3,2,1,0:T(8,128)} copy(f32[2,2,128,128]{3,2,1,0:T(8,128)S(1)} %bitcast.1) | data formatting | bytes 524288
